TPU v7x, 256 devices: a whole 4x4x8 slice. The times are simulated.
256 devices in a mesh: grp: 4 (over z_hi), dev: 64 (over z_lo, y, x, core).
Axes of the slice: x: 4, y: 4, z: 8 (z_hi: 4, z_lo: 2; z = z_hi * 2 + z_lo), core: 2. Of those that a mesh axis runs over, the one named last changes fastest.
Arguments:
- series: float32 [2, 33554432], P(None, ('grp', 'dev')), may hold values from -6 to 6
Outputs:
- spectrum: float32 [2, 33554432], P(None, ('grp', 'dev'))
All inputs are finite; a program needn't handle non-finite values.
Results may differ from a plain program's by a relative error of at most 0.00007.
Values sent between devices are 32-bit elements; how exact they have to be, the bound alone decides.
A program may use at most 128 MiB of HBM per device.

v0:
```python
import math

import jax
import jax.numpy as jnp
import ml_dtypes
import numpy as np
from jax import lax
from jax.experimental import pallas as pl
from jax.experimental.pallas import tpu as pltpu
from jax.sharding import PartitionSpec as P

MESH = pl.DeviceIdType.MESH
BITS = 25
LANES = 128
PEERS = 256
CHUNKS = 4
ROWS = 512


def split(table):
    high = table.astype(ml_dtypes.bfloat16)
    low = (table - high.astype(np.float64)).astype(ml_dtypes.bfloat16)
    return np.stack([high, low])


def table_256():
    at = np.arange(256)
    angle = 2.0 * np.pi * ((at[:, None] * at[None, :]) % 256) / 256
    cosine, sine = np.cos(angle), np.sin(angle)
    full = np.zeros((2, 256, 256, 2))
    full[0, :, :, 0], full[0, :, :, 1] = cosine, sine
    full[1, :, :, 0], full[1, :, :, 1] = -sine, cosine
    return split(full.reshape(512, 512))


def table_512():
    at = np.arange(512)
    angle = 2.0 * np.pi * ((at[:, None] * at[None, :]) % 512) / 512
    cosine, sine = np.cos(angle), np.sin(angle)
    full = np.zeros((256, 2, 2, 2, 512))
    cosine, sine = cosine.reshape(256, 2, 512), sine.reshape(256, 2, 512)
    full[:, :, 0, 0], full[:, :, 0, 1] = cosine, sine
    full[:, :, 1, 0], full[:, :, 1, 1] = -sine, cosine
    full = full.transpose(1, 0, 2, 3, 4).reshape(2, 512, 1024)
    return split(full)


def turn(steps):
    quarter = (steps + (1 << (BITS - 3))) >> (BITS - 2)
    rest = steps - (quarter << (BITS - 2))
    x = rest.astype(jnp.float32) * (2.0 * math.pi / (1 << BITS))
    y = x * x
    sine = x * (1.0 + y * (-1.0 / 6 + y * (1.0 / 120 + y * (-1.0 / 5040 + y * (1.0 / 362880)))))
    cosine = 1.0 + y * (-0.5 + y * (1.0 / 24 + y * (-1.0 / 720 + y * (1.0 / 40320))))
    odd = (quarter & 1) != 0
    c, s = jnp.where(odd, sine, cosine), jnp.where(odd, cosine, sine)
    c = jnp.where(((quarter + 1) & 2) != 0, -c, c)
    s = jnp.where((quarter & 2) != 0, -s, s)
    return c, s


def shifted(me, i):
    z, y, x, c = me >> 5, (me >> 3) & 3, (me >> 1) & 3, me & 1
    z = (z + (i & 7)) & 7
    c = c ^ ((i >> 3) & 1)
    x = (x + ((i >> 4) & 3)) & 3
    y = (y + ((i >> 6) & 3)) & 3
    return z * 32 + y * 8 + x * 2 + c


def address(device):
    return (device >> 6, device & 63)


def halves(values):
    high = values.astype(jnp.bfloat16)
    return high, (values - high.astype(jnp.float32)).astype(jnp.bfloat16)


def dot(a, b):
    return jnp.dot(a, b, preferred_element_type=jnp.float32)


def dot_t(a, b):
    return lax.dot_general(a, b, (((1,), (1,)), ((), ())), preferred_element_type=jnp.float32)


def kernel(
    x_ref, a_hbm, b_hbm, o_ref,
    r1, s2, r2, s3, r3, out, zb, a, b, t1, t2,
    load_sem, out_sem, ready, self_sem, send_sem, recv_sem,
):
    me = lax.axis_index("grp") * 64 + lax.axis_index("dev")

    barrier = pltpu.get_barrier_semaphore()

    def greet_column(i, carry):
        pl.semaphore_signal(barrier, inc=1, device_id=address(shifted(me, i + 1)), device_id_type=MESH)
        return carry

    def greet_plane(i, carry):
        pl.semaphore_signal(barrier, inc=1, device_id=address(shifted(me, (i + 1) * 8)), device_id_type=MESH)
        return carry

    lax.fori_loop(0, 7, greet_column, 0)
    lax.fori_loop(0, 31, greet_plane, 0)

    load_a = pltpu.make_async_copy(a_hbm, a, load_sem.at[0])
    load_b = pltpu.make_async_copy(b_hbm, b, load_sem.at[1])
    load_a.start()
    load_b.start()

    scale = 1.0 / math.sqrt(1 << BITS)

    def fill(table, row_step, column_start, factor):
        def block(i, carry):
            start = pl.multiple_of(i * 16, 16)
            row = lax.broadcasted_iota(jnp.int32, (16, 512), 0) + start
            column = lax.broadcasted_iota(jnp.int32, (16, 512), 1) + column_start
            c, s = turn(row * column * row_step)
            if factor is not None:
                c, s = c * factor, s * factor
            table[0, pl.ds(start, 16), :] = c
            table[1, pl.ds(start, 16), :] = s
            return carry

        lax.fori_loop(0, 16, block, 0)

    fill(t1, 1, me * 512, scale)

    pl.semaphore_wait(barrier, 38)

    def tell_column(i, carry):
        pl.semaphore_signal(ready, inc=1, device_id=address(shifted(me, i + 1)), device_id_type=MESH)
        return carry

    lax.fori_loop(0, 7, tell_column, 0)
    pl.semaphore_wait(ready, 7)

    def exchange(phase, chunk, source, first, step, target):
        at = phase * CHUNKS + chunk
        own = target.at[pl.ds(chunk * ROWS + me * 2, 2)]

        def send(i, carry):
            other = shifted(me, i + 1)
            pltpu.make_async_remote_copy(
                src_ref=source.at[pl.ds(first + other * step, 2)],
                dst_ref=own,
                send_sem=send_sem.at[at],
                recv_sem=recv_sem.at[at],
                device_id=address(other),
                device_id_type=MESH,
            ).start()
            return carry

        lax.fori_loop(0, PEERS - 1, send, 0)
        pltpu.make_async_copy(source.at[pl.ds(first + me * step, 2)], own, self_sem.at[at]).start()

    def arrived(phase, chunk, target):
        at = phase * CHUNKS + chunk
        rest = target.at[pl.ds(chunk * ROWS, ROWS - 2)]
        one = target.at[pl.ds(chunk * ROWS, 2)]
        pltpu.make_async_copy(one, one, self_sem.at[at]).wait()
        pltpu.make_async_copy(rest, rest, recv_sem.at[at]).wait()

    for q in range(CHUNKS):
        exchange(0, q, x_ref, q * 2, 8, r1)

    fill(t2, 256, 0, None)
    load_a.wait()
    load_b.wait()

    def sum_256(values):
        high, low = halves(values)
        total = dot(a[0], high) + dot(a[0], low) + dot(a[1], high)
        return total[:256], total[256:]

    def rotate(real, imag, table, q):
        c = table[0, :, q * LANES : (q + 1) * LANES]
        s = table[1, :, q * LANES : (q + 1) * LANES]
        return real * c + imag * s, imag * c - real * s

    for q in range(CHUNKS):
        arrived(0, q, r1)
        real, imag = sum_256(r1[q * ROWS : (q + 1) * ROWS, :])
        real, imag = rotate(real, imag, t1, q)
        s2[pl.ds(q * ROWS, 256, stride=2), :] = real
        s2[pl.ds(q * ROWS + 1, 256, stride=2), :] = imag
        exchange(1, q, s2, q * ROWS, 2, r2)

    for q in range(CHUNKS):
        arrived(1, q, r2)
        real, imag = sum_256(r2[q * ROWS : (q + 1) * ROWS, :])
        parts = rotate(real, imag, t2, q)
        for part in range(2):
            columns = slice(part * 512 + q * LANES, part * 512 + (q + 1) * LANES)
            high, low = halves(parts[part])
            for side in range(2):
                zb[side, 0:128, columns] = high[side * 128 : (side + 1) * 128]
                zb[side, 128:256, columns] = low[side * 128 : (side + 1) * 128]

    for h in range(CHUNKS):
        odd, side = h // 2, h % 2
        both = dot_t(b[0, odd], zb[side])
        s3[h * ROWS : (h + 1) * ROWS, :] = (
            both[:, :128] + both[:, 128:] + dot_t(b[1, odd], zb[side, 0:128, :])
        )
        exchange(2, h, s3, h * ROWS, 2, r3)

    for h in range(CHUNKS):
        arrived(2, h, r3)
        for part in range(2):
            flipped = r3[pl.ds(h * ROWS + part, 256, stride=2), :].T
            out[pl.ds(h * ROWS + part, 128, stride=4), :] = flipped[:, :128]
            out[pl.ds(h * ROWS + 2 + part, 128, stride=4), :] = flipped[:, 128:]
        rows = pl.ds(h * ROWS, ROWS)
        pltpu.make_async_copy(out.at[rows], o_ref.at[rows], out_sem.at[h]).start()

    for h in range(CHUNKS):
        rows = pl.ds(h * ROWS, ROWS)
        pltpu.make_async_copy(out.at[rows], o_ref.at[rows], out_sem.at[h]).wait()
    for phase, source in enumerate((x_ref, s2, s3)):
        for chunk in range(CHUNKS):
            sent = source.at[pl.ds(0, ROWS - 2)]
            pltpu.make_async_copy(sent, sent, send_sem.at[phase * CHUNKS + chunk]).wait()


def local(series):
    rows = series.reshape(2, 1024, LANES).transpose(1, 0, 2).reshape(2048, LANES)
    big = pltpu.VMEM((2048, LANES), jnp.float32)
    result = pl.pallas_call(
        kernel,
        out_shape=jax.ShapeDtypeStruct((2048, LANES), jnp.float32),
        in_specs=[pl.BlockSpec(memory_space=pl.ANY)] * 3,
        out_specs=pl.BlockSpec(memory_space=pl.ANY),
        scratch_shapes=[
            big, big, big, big, big, big,
            pltpu.VMEM((2, 256, 1024), jnp.bfloat16),
            pltpu.VMEM((2, 512, 512), jnp.bfloat16),
            pltpu.VMEM((2, 2, 512, 1024), jnp.bfloat16),
            pltpu.VMEM((2, 256, 512), jnp.float32),
            pltpu.VMEM((2, 256, 512), jnp.float32),
            pltpu.SemaphoreType.DMA((2,)),
            pltpu.SemaphoreType.DMA((CHUNKS,)),
            pltpu.SemaphoreType.REGULAR,
            pltpu.SemaphoreType.DMA((3 * CHUNKS,)),
            pltpu.SemaphoreType.DMA((3 * CHUNKS,)),
            pltpu.SemaphoreType.DMA((3 * CHUNKS,)),
        ],
        compiler_params=pltpu.CompilerParams(
            collective_id=0, has_side_effects=True, vmem_limit_bytes=56 * 1024 * 1024
        ),
        cost_estimate=pl.CostEstimate(flops=3_000_000_000, bytes_accessed=8_000_000, transcendentals=0),
    )(rows, jnp.asarray(table_256()), jnp.asarray(table_512()))
    return result.reshape(1024, 2, LANES).transpose(1, 0, 2).reshape(2, 131072)


def solution(mesh):
    return jax.shard_map(
        local,
        mesh=mesh,
        in_specs=(P(None, ("grp", "dev")),),
        out_specs=P(None, ("grp", "dev")),
        check_vma=False,
    )
```

profile of v0, /device:TPU:1, one launch (start us, length us, event | category | flops | bytes accessed | tf_op | source)
XLA Modules:
  0.0 96.4 jit_solution(2903606790188831012)
XLA Ops:
  0.0 94.2 %shard_map.37 = f32[2048,128]{1,0:T(8,128)} custom-call(f32[2048,128]{1,0:T(8,128)} %bitcast.11, bf16[2,512,512]{2,1,0:T(8,128)(2,1)} %constant.4.clone.a_hbm, bf16[2,2,512,1024]{3,2,1,0:T(8,128)(2,1)} %constant.5.clone.b_hbm), custom_call_target="tpu_custom_call" | custom-call | flops 3000000000 | bytes 8000000 | tf_op jit(solution)/shard_map/pallas_call | solution.py:231
  94.2 2.3 %copy.7 = f32[2,131072]{1,0:T(2,128)} copy(f32[2,131072]{1,0:T(2,128)} %bitcast.10) | data formatting | bytes 2097152
where the time goes:
time: 96.6 us; the launch traced here: 96.4 us
  Pallas kernels  94.2 us (98%)
  local copies, waits for them, and re-layouts  2.26 us (2%)
    pallas_call x1, Pallas kernels, local(): pl.pallas_call(kernel, out_shape=jax.ShapeDtypeStruct((2048, LANES), jnp....  94.2 us
    unnamed x1, local copies, waits for them, and re-layouts  2.26 us

commit v1 on v0

v1 whole, which is shorter than its diff:
```python
import math

import jax
import jax.numpy as jnp
import ml_dtypes
import numpy as np
from jax import lax
from jax.experimental import pallas as pl
from jax.experimental.pallas import tpu as pltpu
from jax.sharding import PartitionSpec as P

MESH = pl.DeviceIdType.MESH
BITS = 25
LANES = 128
PEERS = 256
CHUNKS = 4
ROWS = 512


def split(table):
    high = table.astype(ml_dtypes.bfloat16)
    low = (table - high.astype(np.float64)).astype(ml_dtypes.bfloat16)
    return np.stack([high, low])


def sum_table(index):
    length = index.size
    angle = 2.0 * np.pi * ((np.arange(length)[:, None] * index[None, :]) % length) / length
    cosine, sine = np.cos(angle), np.sin(angle)
    full = np.zeros((2, length, length, 2))
    full[0, :, :, 0], full[0, :, :, 1] = cosine, sine
    full[1, :, :, 0], full[1, :, :, 1] = -sine, cosine
    return full.reshape(2 * length, 2 * length)


def tables():
    device = np.arange(256)
    first = sum_table(np.concatenate([device * 2, device * 2 + 1]))
    first = first.reshape(2, 2, 256, 1024).transpose(1, 0, 2, 3).reshape(1024, 1024)
    second = sum_table(np.arange(512))
    third = sum_table(np.arange(128)).reshape(256, 128, 2).transpose(0, 2, 1).reshape(256, 256)
    return split(first), split(second), split(third)


def turn(steps):
    quarter = (steps + (1 << (BITS - 3))) >> (BITS - 2)
    rest = steps - (quarter << (BITS - 2))
    x = rest.astype(jnp.float32) * (2.0 * math.pi / (1 << BITS))
    y = x * x
    sine = x * (1.0 + y * (-1.0 / 6 + y * (1.0 / 120 + y * (-1.0 / 5040 + y * (1.0 / 362880)))))
    cosine = 1.0 + y * (-0.5 + y * (1.0 / 24 + y * (-1.0 / 720 + y * (1.0 / 40320))))
    odd = (quarter & 1) != 0
    c, s = jnp.where(odd, sine, cosine), jnp.where(odd, cosine, sine)
    c = jnp.where(((quarter + 1) & 2) != 0, -c, c)
    s = jnp.where((quarter & 2) != 0, -s, s)
    return c, s


def shifted(me, i):
    z, y, x, c = me >> 5, (me >> 3) & 3, (me >> 1) & 3, me & 1
    z = (z + (i & 7)) & 7
    c = c ^ ((i >> 3) & 1)
    x = (x + ((i >> 4) & 3)) & 3
    y = (y + ((i >> 6) & 3)) & 3
    return z * 32 + y * 8 + x * 2 + c


def address(device):
    return (device >> 6, device & 63)


def halves(values):
    high = values.astype(jnp.bfloat16)
    return high, (values - high.astype(jnp.float32)).astype(jnp.bfloat16)


def dot(a, b):
    return jnp.dot(a, b, preferred_element_type=jnp.float32)


def dot_t(a, b):
    return lax.dot_general(a, b, (((1,), (1,)), ((), ())), preferred_element_type=jnp.float32)


def kernel(
    x_ref, a_hbm, b_hbm, c_hbm, o_ref,
    xs, r0, r1, s2, r2, s3, r3, out, zb, acc, a, b, c, t1, t2,
    load_sem, out_sem, ready, self_sem, send_sem, recv_sem,
):
    me = lax.axis_index("grp") * 64 + lax.axis_index("dev")
    plane, spot = me >> 5, me & 31

    barrier = pltpu.get_barrier_semaphore()

    def greet(i, carry):
        pl.semaphore_signal(barrier, inc=1, device_id=address(shifted(me, i)), device_id_type=MESH)
        return carry

    lax.fori_loop(1, 8, greet, 0)
    lax.fori_loop(1, 32, lambda i, carry: greet(i * 8, carry), 0)

    loads = [
        pltpu.make_async_copy(x_ref.at[pl.ds((n16 * 2 + q) * ROWS, ROWS)], xs.at[q * 2 + n16], load_sem.at[q * 2 + n16])
        for q in range(2)
        for n16 in range(2)
    ]
    loads += [
        pltpu.make_async_copy(source, target, load_sem.at[4 + i])
        for i, (source, target) in enumerate(((a_hbm, a), (b_hbm, b), (c_hbm, c)))
    ]
    for load in loads:
        load.start()

    def fill(table, width, entry):
        lane = lax.broadcasted_iota(jnp.int32, (16, LANES), 1)

        def block(i, carry):
            start = pl.multiple_of(i * 16, 16)
            row = lax.broadcasted_iota(jnp.int32, (16, LANES), 0) + start
            for q in range(width):
                cosine, sine = turn(entry(row, q, lane))
                table[0, pl.ds(start, 16), q * LANES : (q + 1) * LANES] = cosine
                table[1, pl.ds(start, 16), q * LANES : (q + 1) * LANES] = sine
            return carry

        lax.fori_loop(0, 32, block, 0)

    fill(t1, 2, lambda row, q, lane: row * (q * 32768 + me * 128 + lane))

    for load in loads[:4]:
        load.wait()
    pl.semaphore_wait(barrier, 38)

    def remote(source, target, device, at):
        pltpu.make_async_remote_copy(
            src_ref=source,
            dst_ref=target,
            send_sem=send_sem.at[at],
            recv_sem=recv_sem.at[at],
            device_id=address(device),
            device_id_type=MESH,
        ).start()

    def finished(like, semaphore):
        pltpu.make_async_copy(like, like, semaphore).wait()

    def along_z():
        own = r0.at[plane]

        def send(i, carry):
            other = shifted(me, i)
            remote(xs.at[2, pl.ds((other >> 5) * 64, 64)], own, other, 0)
            return carry

        lax.fori_loop(1, 8, send, 0)
        pltpu.make_async_copy(xs.at[2, pl.ds(plane * 64, 64)], own, self_sem.at[0]).start()

    def in_plane():
        finished(r0.at[0], self_sem.at[0])
        finished(r0.at[pl.ds(0, 7)], recv_sem.at[0])
        own = r1.at[2, :, pl.ds(spot * 2, 2)]

        def send(i, carry):
            other = shifted(me, i * 8)
            remote(r0.at[:, pl.ds((other & 31) * 2, 2)], own, other, 1)
            return carry

        lax.fori_loop(1, 32, send, 0)
        pltpu.make_async_copy(r0.at[:, pl.ds(spot * 2, 2)], own, self_sem.at[1]).start()

    def in_plane_done():
        finished(xs.at[0, pl.ds(0, 16)], self_sem.at[1])
        finished(xs.at[0, pl.ds(0, ROWS - 16)], recv_sem.at[1])

    def exchange(at, source, own):
        def send(i, carry):
            other = shifted(me, i)
            remote(source(other), own, other, at)
            return carry

        lax.fori_loop(1, PEERS, send, 0, unroll=5)
        pltpu.make_async_copy(source(me), own, self_sem.at[at]).start()

    def arrived(at, rows, target):
        finished(xs.at[0, pl.ds(0, rows)], self_sem.at[at])
        finished(target, recv_sem.at[at])

    def product(table, rows, columns, values):
        high, low = halves(values)
        return dot(table[0, rows, columns], high) + dot(table[0, rows, columns], low) + dot(table[1, rows, columns], high)

    everything, half = slice(0, 1024), (slice(0, 512), slice(512, 1024))

    def rotate(real, imag, cosine, sine):
        return real * cosine + imag * sine, imag * cosine - real * sine

    def first_sum(k8, q, total):
        rows, lanes = slice(k8 * 256, (k8 + 1) * 256), slice(q * LANES, (q + 1) * LANES)
        real, imag = rotate(total[:256], total[256:], t1[0, rows, lanes], t1[1, rows, lanes])
        s2[k8 * 2 + q, pl.ds(0, 256, stride=2), :] = real
        s2[k8 * 2 + q, pl.ds(1, 256, stride=2), :] = imag

    def first_whole(k8, q):
        first_sum(k8, q, product(a, half[k8], everything, r1[q * 2 : q * 2 + 2].reshape(1024, LANES)))

    def second_sum(total):
        for part, values in enumerate(rotate(total[:512], total[512:], t2[0], t2[1])):
            lanes = slice(part * LANES, (part + 1) * LANES)
            zb[0, :, lanes], zb[1, :, lanes] = halves(values)

    def third_sum(k8, k16):
        for k17 in range(2):
            rows = slice((k17 * 2 + k16) * LANES, (k17 * 2 + k16 + 1) * LANES)
            total = dot_t(c[0], zb[0, rows]) + dot_t(c[0], zb[1, rows]) + dot_t(c[1], zb[0, rows])
            for part in range(2):
                s3[k8 * 2 + k16, pl.ds(k17 * 2 + part, 128, stride=4), :] = total[part * 128 : (part + 1) * 128]

    def tell(i, carry):
        pl.semaphore_signal(ready, inc=1, device_id=address(shifted(me, i)), device_id_type=MESH)
        return carry

    def pair(buffer, chunk, count):
        def of(device):
            return buffer.at[pl.ds(chunk, count), pl.ds(device * 2, 2)]

        return of

    most = xs.at[0, pl.ds(0, ROWS - 2)]
    two = xs.at[pl.ds(0, 2), pl.ds(0, ROWS - 2)]

    lax.fori_loop(1, 8, tell, 0)
    along_z()
    pl.semaphore_wait(ready, 7)
    exchange(2, pair(xs, 0, 2), r1.at[pl.ds(0, 2), plane, pl.ds(spot * 2, 2)])
    in_plane()
    exchange(3, pair(xs, 3, 1), r1.at[pl.ds(3, 1), plane, pl.ds(spot * 2, 2)])
    fill(t2, 1, lambda row, q, lane: row * lane * 512)
    for load in loads[4:]:
        load.wait()
    arrived(2, 4, two)
    first_whole(0, 0)
    exchange(4, pair(s2, 0, 1), pair(r2, 0, 1)(me))
    in_plane_done()
    acc[0:512, :] = product(a, half[0], half[0], r1[2].reshape(512, LANES))
    arrived(3, 2, most)
    first_sum(0, 1, acc[0:512, :] + product(a, half[0], half[1], r1[3].reshape(512, LANES)))
    exchange(5, pair(s2, 1, 1), pair(r2, 1, 1)(me))
    first_whole(1, 0)
    first_whole(1, 1)
    exchange(6, pair(s2, 2, 2), pair(r2, 2, 2)(me))
    arrived(4, 2, most)
    acc[...] = product(b, everything, half[0], r2[0])
    arrived(5, 2, most)
    second_sum(acc[...] + product(b, everything, half[1], r2[1]))
    third_sum(0, 0)
    exchange(7, pair(s3, 0, 1), pair(r3, 0, 1)(me))
    third_sum(0, 1)
    exchange(8, pair(s3, 1, 1), pair(r3, 1, 1)(me))
    arrived(6, 4, two)
    second_sum(product(b, everything, everything, r2[2:4].reshape(1024, LANES)))
    third_sum(1, 0)
    exchange(9, pair(s3, 2, 1), pair(r3, 2, 1)(me))
    third_sum(1, 1)
    exchange(10, pair(s3, 3, 1), pair(r3, 3, 1)(me))

    def store(k16):
        rows = pl.ds(k16 * 1024, 1024)
        return pltpu.make_async_copy(out.at[rows], o_ref.at[rows], out_sem.at[k16])

    for k8 in range(2):
        for k16 in range(2):
            chunk = k8 * 2 + k16
            arrived(7 + chunk, 2, most)
            for part in range(2):
                flipped = r3[chunk, pl.ds(part, 256, stride=2), :].T
                first = k16 * 1024 + k8 * 4 + part
                out[pl.ds(first, 128, stride=8), :] = flipped[:, :128]
                out[pl.ds(first + 2, 128, stride=8), :] = flipped[:, 128:]
            if k8 == 1:
                store(k16).start()

    for k16 in range(2):
        store(k16).wait()
    finished(xs.at[0, pl.ds(0, ROWS - 64)], send_sem.at[0])
    finished(xs.at[0, pl.ds(0, ROWS - 16)], send_sem.at[1])
    for at in range(2, 11):
        finished(two if at in (2, 6) else most, send_sem.at[at])


def local(series):
    rows = series.reshape(2, 1024, LANES).transpose(1, 0, 2).reshape(2048, LANES)
    chunks = pltpu.VMEM((CHUNKS, ROWS, LANES), jnp.float32)
    result = pl.pallas_call(
        kernel,
        out_shape=jax.ShapeDtypeStruct((2048, LANES), jnp.float32),
        in_specs=[pl.BlockSpec(memory_space=pl.ANY)] * 4,
        out_specs=pl.BlockSpec(memory_space=pl.ANY),
        scratch_shapes=[
            chunks,
            pltpu.VMEM((8, 64, LANES), jnp.float32),
            pltpu.VMEM((4, 8, 64, LANES), jnp.float32),
            chunks, chunks, chunks, chunks,
            pltpu.VMEM((2048, LANES), jnp.float32),
            pltpu.VMEM((2, 512, 256), jnp.bfloat16),
            pltpu.VMEM((1024, LANES), jnp.float32),
            pltpu.VMEM((2, 1024, 1024), jnp.bfloat16),
            pltpu.VMEM((2, 1024, 1024), jnp.bfloat16),
            pltpu.VMEM((2, 256, 256), jnp.bfloat16),
            pltpu.VMEM((2, 512, 256), jnp.float32),
            pltpu.VMEM((2, 512, 128), jnp.float32),
            pltpu.SemaphoreType.DMA((7,)),
            pltpu.SemaphoreType.DMA((2,)),
            pltpu.SemaphoreType.REGULAR,
            pltpu.SemaphoreType.DMA((11,)),
            pltpu.SemaphoreType.DMA((11,)),
            pltpu.SemaphoreType.DMA((11,)),
        ],
        compiler_params=pltpu.CompilerParams(
            collective_id=0, has_side_effects=True, vmem_limit_bytes=56 * 1024 * 1024
        ),
        cost_estimate=pl.CostEstimate(flops=3_000_000_000, bytes_accessed=8_000_000, transcendentals=0),
    )(rows, *(jnp.asarray(table) for table in tables()))
    result = result * (1.0 / math.sqrt(1 << BITS))
    return result.reshape(1024, 2, LANES).transpose(1, 0, 2).reshape(2, 131072)


def solution(mesh):
    return jax.shard_map(
        local,
        mesh=mesh,
        in_specs=(P(None, ("grp", "dev")),),
        out_specs=P(None, ("grp", "dev")),
        check_vma=False,
    )
```

time: 96.6 us -> 88.7 us (0.918)
  Pallas kernels: 94.2 us -> 86.3 us
  other arithmetic: 0 us -> 2.29 us
  local copies, waits for them, and re-layouts: 2.26 us -> 0 us
    pallas_call x1, Pallas kernels: 94.2 us -> 86.3 us  [local(): pl.pallas_call(kernel, out_shape=jax.ShapeDtypeStruct((2048, LANES), jnp....]
    mul x0 -> x1, other arithmetic: none -> 2.29 us  [local(): result = result * (1.0 / math.sqrt(1 << BITS))]
    unnamed x1 -> x0, local copies, waits for them, and re-layouts: 2.26 us -> none
where the time goes in v1:
time: 88.7 us; the launch traced here: 88.6 us
  Pallas kernels  86.3 us (97%)
  other arithmetic  2.29 us (3%)
    pallas_call x1, Pallas kernels, local(): pl.pallas_call(kernel, out_shape=jax.ShapeDtypeStruct((2048, LANES), jnp....  86.3 us
    mul x1, other arithmetic, local(): result = result * (1.0 / math.sqrt(1 << BITS))  2.29 us

profile of v1, /device:TPU:1, one launch (start us, length us, event | category | flops | bytes accessed | tf_op | source)
XLA Modules:
  0.0 88.6 jit_solution(14872155101245185863)
XLA Ops:
  0.0 86.3 %shard_map.46 = f32[2048,128]{1,0:T(8,128)} custom-call(f32[2048,128]{1,0:T(8,128)} %bitcast.10, bf16[2,1024,1024]{2,1,0:T(8,128)(2,1)} %constant.8.clone.a_hbm, bf16[2,1024,1024]{2,1,0:T(8,128)(2,1)} %constant.9.clone.b_hbm, bf16[2,256,256]{2,1,0:T(8,128)(2,1)} %constant.10.clone.c_hbm), custom_call_target="tpu_custom_call" | custom-call | flops 3000000000 | bytes 8000000 | tf_op jit(solution)/shard_map/pallas_call | solution.py:293
  86.3 2.3 %broadcast_multiply_fusion = f32[2048,128]{1,0:T(8,128)} fusion(f32[2048,128]{1,0:T(8,128)} %shard_map.46), kind=kLoop, calls=%fused_computation | loop fusion | flops 262144 | bytes 2097152 | tf_op jit(solution)/shard_map/mul | solution.py:323

commit v2 on v1

--- a/solution.py
+++ b/solution.py
@@ -39,7 +39,7 @@
     first = first.reshape(2, 2, 256, 1024).transpose(1, 0, 2, 3).reshape(1024, 1024)
     second = sum_table(np.arange(512))
     third = sum_table(np.arange(128)).reshape(256, 128, 2).transpose(0, 2, 1).reshape(256, 256)
-    return split(first), split(second), split(third)
+    return split(np.concatenate([first, second, np.pad(third, ((0, 0), (0, 768)))]))
 
 
 def turn(steps):
@@ -83,7 +83,7 @@
 
 
 def kernel(
-    x_ref, a_hbm, b_hbm, c_hbm, o_ref,
+    x_ref, tables_ref, o_ref,
     xs, r0, r1, s2, r2, s3, r3, out, zb, acc, a, b, c, t1, t2,
     load_sem, out_sem, ready, self_sem, send_sem, recv_sem,
 ):
@@ -106,7 +106,13 @@
     ]
     loads += [
         pltpu.make_async_copy(source, target, load_sem.at[4 + i])
-        for i, (source, target) in enumerate(((a_hbm, a), (b_hbm, b), (c_hbm, c)))
+        for i, (source, target) in enumerate(
+            (
+                (tables_ref.at[:, pl.ds(0, 1024)], a),
+                (tables_ref.at[:, pl.ds(1024, 1024)], b),
+                (tables_ref.at[:, pl.ds(2048, 256), pl.ds(0, 256)], c),
+            )
+        )
     ]
     for load in loads:
         load.start()
@@ -293,7 +299,7 @@
     result = pl.pallas_call(
         kernel,
         out_shape=jax.ShapeDtypeStruct((2048, LANES), jnp.float32),
-        in_specs=[pl.BlockSpec(memory_space=pl.ANY)] * 4,
+        in_specs=[pl.BlockSpec(memory_space=pl.ANY)] * 2,
         out_specs=pl.BlockSpec(memory_space=pl.ANY),
         scratch_shapes=[
             chunks,
@@ -316,10 +322,10 @@
             pltpu.SemaphoreType.DMA((11,)),
         ],
         compiler_params=pltpu.CompilerParams(
-            collective_id=0, has_side_effects=True, vmem_limit_bytes=56 * 1024 * 1024
+            collective_id=0, has_side_effects=True, vmem_limit_bytes=52 * 1024 * 1024
         ),
         cost_estimate=pl.CostEstimate(flops=3_000_000_000, bytes_accessed=8_000_000, transcendentals=0),
-    )(rows, *(jnp.asarray(table) for table in tables()))
+    )(rows, jnp.asarray(tables()))
     result = result * (1.0 / math.sqrt(1 << BITS))
     return result.reshape(1024, 2, LANES).transpose(1, 0, 2).reshape(2, 131072)
 

time: 88.7 us -> 86.7 us (0.977)
  other arithmetic: 2.29 us -> 1.06 us
    mul x1, other arithmetic: 2.29 us -> 1.06 us  [local(): result = result * (1.0 / math.sqrt(1 << BITS))]
where the time goes in v2:
time: 86.7 us; the launch traced here: 86.6 us
  Pallas kernels  85.6 us (99%)
  other arithmetic  1.06 us (1%)
    pallas_call x1, Pallas kernels, local(): pl.pallas_call(kernel, out_shape=jax.ShapeDtypeStruct((2048, LANES), jnp....  85.6 us

profile of v2, /device:TPU:1, one launch (start us, length us, event | category | flops | bytes accessed | tf_op | source)
XLA Modules:
  0.0 86.6 jit_solution(6495661454450457401)
XLA Ops:
  0.0 85.6 %shard_map.28 = f32[2048,128]{1,0:T(8,128)S(1)} custom-call(f32[2048,128]{1,0:T(8,128)} %bitcast.10, bf16[2,2304,1024]{2,1,0:T(8,128)(2,1)} %constant.4.clone.tables_ref), custom_call_target="tpu_custom_call" | custom-call | flops 3000000000 | bytes 8000000 | tf_op jit(solution)/shard_map/pallas_call | solution.py:299
  85.6 1.1 %broadcast_multiply_fusion = f32[2048,128]{1,0:T(8,128)} fusion(f32[2048,128]{1,0:T(8,128)S(1)} %shard_map.28), kind=kLoop, calls=%fused_computation | loop fusion | flops 262144 | bytes 2097152 | tf_op jit(solution)/shard_map/mul | solution.py:329
